TPU v7x, 32 devices: a whole 2x2x4 slice. The times are simulated.
32 devices in a mesh: row: 4 (over z), col: 4 (over y, x), filt: 2 (over core).
Axes of the slice: x: 2, y: 2, z: 4, core: 2. Of those that a mesh axis runs over, the one named last changes fastest.
Arguments:
- grad_out: bfloat16 [16, 128, 64, 256], P(None, 'row', 'col', 'filt'), may hold values from -6 to 6
- pre_act: bfloat16 [16, 128, 64, 256], P(None, 'row', 'col', 'filt'), may hold values from -6 to 6
- weight_one: bfloat16 [3, 3, 256, 256], replicated, may hold values from -0.125 to 0.125
- weight_two: bfloat16 [3, 3, 256, 256], replicated, may hold values from -0.125 to 0.125
Outputs:
- grad_in: bfloat16 [16, 128, 64, 256], P(None, 'row', 'col', 'filt')
All inputs are finite; a program needn't handle non-finite values.
Results may differ from a plain program's by a relative error of at most 0.0049.
Values may be sent and summed in bfloat16 or wider, within the bound.
A program may use at most 192 MiB of HBM per device.

v0:
```python
import jax
import jax.numpy as jnp
from jax import lax
from jax.sharding import PartitionSpec as P


def padded_2(cells, sides, width):
    for axis, dim in sides:
        count = lax.axis_size(axis)
        ends = count - 1
        head = lax.slice_in_dim(cells, 0, width, axis=dim)
        tail = lax.slice_in_dim(cells, cells.shape[dim] - width, cells.shape[dim], axis=dim)
        cells = jnp.concatenate(
            [
                lax.ppermute(tail, axis, [(i, (i + 1) % count) for i in range(ends)]),
                cells,
                lax.ppermute(head, axis, [((i + 1) % count, i) for i in range(ends)]),
            ],
            axis=dim,
        )
    return cells


def tap_sum(padded, weight, spacing, rows, cols):
    total = None
    for tap_row in range(3):
        for tap_col in range(3):
            top = spacing * (2 - tap_row)
            left = spacing * (2 - tap_col)
            piece = padded[:, top : top + rows, left : left + cols, :]
            term = jnp.einsum(
                "bhwo,io->bhwi", piece, weight[tap_row, tap_col], preferred_element_type=jnp.float32
            )
            total = term if total is None else total + term
    return total


def per_device(grad_out, pre_act, weight_one, weight_two):
    rows = grad_out.shape[1]
    cols = grad_out.shape[2]
    own_width = grad_out.shape[3]
    first_channel = lax.axis_index("filt") * own_width
    outer = padded_2(grad_out, (("row", 1), ("col", 2)), 4)
    cols_two = lax.dynamic_slice_in_dim(weight_two, first_channel, own_width, 3)
    grad_a = lax.psum_scatter(
        tap_sum(outer, cols_two, 4, rows, cols), "filt", scatter_dimension=3, tiled=True
    )
    grad_h = jnp.where(pre_act > 0, grad_a, jnp.float32(0.0)).astype(jnp.bfloat16)
    inner = padded_2(grad_h, (("row", 1), ("col", 2)), 2)
    cols_one = lax.dynamic_slice_in_dim(weight_one, first_channel, own_width, 3)
    grad_in = lax.psum_scatter(
        tap_sum(inner, cols_one, 2, rows, cols), "filt", scatter_dimension=3, tiled=True
    )
    return grad_in.astype(jnp.bfloat16)


def solution(mesh):
    placed = (P(None, "row", "col", "filt"), P(None, "row", "col", "filt"), P(), P())
    return jax.shard_map(
        per_device,
        mesh=mesh,
        in_specs=placed,
        out_specs=P(None, "row", "col", "filt"),
        check_vma=False,
    )
```

profile of v0, /device:TPU:0, one launch (start us, length us, event | category | flops | bytes accessed | tf_op | source)
XLA Modules:
  0.0 230.0 jit_solution(10505227247822113965)
XLA Ops:
  8.4 4.9 %collective-permute-start = (bf16[16,4,16,128]{3,2,1,0:T(8,128)(2,1)S(1)}, bf16[16,4,16,128]{3,2,1,0:T(8,128)(2,1)S(1)}, u32[]{:S(2)}, u32[]{:S(2)}) collective-permute-start(bf16[16,4,16,128]{3,2,1,0:T(8,128)(2,1)S(1)} %get-tuple-element.14), channel_id=1, source_target_pairs={{0,8},{8,16},{16,24},{1,9},{9,17},{17,25},{2,10},{10,18},{18,26},{... | collective-permute-start | bytes 786440 | tf_op jit(solution)/shard_map/ppermute | solution.py:15
  27.4 4.2 %collective-permute-start.3 = (bf16[16,40,4,128]{3,2,1,0:T(4,128)(2,1)}, bf16[16,40,4,128]{3,2,1,0:T(4,128)(2,1)}, u32[]{:S(2)}, u32[]{:S(2)}) collective-permute-start(bf16[16,40,4,128]{3,2,1,0:T(4,128)(2,1)} %get-tuple-element.5), channel_id=1, source_target_pairs={{0,2},{2,4},{4,6},{1,3},{3,5},{5,7},{8,10},{10,12},{12,14},{9,11},... | collective-permute-start | bytes 1966088 | tf_op jit(solution)/shard_map/ppermute | solution.py:15
  31.6 4.5 %fusion.51 = f32[256,16,32,16]{0,3,2,1:T(8,128)} fusion(bf16[16,32,16,128]{3,2,1,0:T(8,128)(2,1)S(1)} %copy-done.4, bf16[3,3,256,256]{3,2,1,0:T(8,128)(2,1)S(1)} %copy-done, s32[]{:T(128)S(6)} %add.73, s32[]{:T(128)S(6)} %select_n.8), kind=kOutput, calls=%fused_computation.77 | convolution fusion | flops 536870912 | bytes 10551304 | tf_op jit(solution)/shard_map/bhwo,io->bhwi/dot_general | solution.py:31
  37.6 5.5 %fusion.4 = f32[16,32,16,256]{3,2,1,0:T(8,128)} fusion(bf16[16,4,16,128]{3,2,1,0:T(8,128)(2,1)} %collective-permute-done.1, bf16[16,32,16,128]{3,2,1,0:T(8,128)(2,1)S(1)} %copy-done.4, bf16[3,3,256,256]{3,2,1,0:T(8,128)(2,1)S(1)} %copy-done, s32[]{:T(128)S(6)} %add.73, s32[]{:T(128)S(6)} %select_n.8), kind=kOutput, calls=%fused_computation.17 | convolution fusion | flops 541589504 | bytes 10813448 | tf_op jit(solution)/shard_map/bhwo,io->bhwi/dot_general | solution.py:31
  43.0 4.5 %fusion.8 = f32[16,32,16,256]{3,2,1,0:T(8,128)} fusion(bf16[16,32,16,128]{3,2,1,0:T(8,128)(2,1)S(1)} %copy-done.4, bf16[16,4,16,128]{3,2,1,0:T(8,128)(2,1)S(1)} %collective-permute-done, bf16[3,3,256,256]{3,2,1,0:T(8,128)(2,1)S(1)} %copy-done, s32[]{:T(128)S(6)} %add.74, s32[]{:T(128)S(6)} %add.73, s32[]{:T(128)S(6)} %select_n.8), kind=kOutput, calls=%fused_computation.21 | convolution fusion | flops 541589504 | bytes 10813452 | tf_op jit(solution)/shard_map/bhwo,io->bhwi/dot_general | solution.py:31
  47.5 5.6 %fusion.21 = f32[16,32,16,256]{3,2,1,0:T(8,128)} fusion(bf16[16,40,16,128]{3,2,1,0:T(8,128)(2,1)S(1)} %copy-done.3, bf16[16,40,4,128]{3,2,1,0:T(4,128)(2,1)} %collective-permute-done.3, bf16[3,3,256,256]{3,2,1,0:T(8,128)(2,1)S(1)} %copy-done, s32[]{:T(128)S(6)} %add.73, s32[]{:T(128)S(6)} %add.74, s32[]{:T(128)S(6)} %select_n.8), kind=kOutput, calls=%fused_computation.34 | convolution fusion | flops 541065216 | bytes 11730956 | tf_op jit(solution)/shard_map/bhwo,io->bhwi/dot_general | solution.py:31
  53.1 5.6 %fusion.24 = f32[16,32,16,256]{3,2,1,0:T(8,128)} fusion(bf16[16,40,16,128]{3,2,1,0:T(8,128)(2,1)S(1)} %copy-done.3, bf16[16,40,4,128]{3,2,1,0:T(4,128)(2,1)} %collective-permute-done.3, bf16[3,3,256,256]{3,2,1,0:T(8,128)(2,1)S(1)} %copy-done, s32[]{:T(128)S(6)} %add.74, s32[]{:T(128)S(6)} %select_n.8), kind=kOutput, calls=%fused_computation.36 | convolution fusion | flops 541065216 | bytes 11730952 | tf_op jit(solution)/shard_map/bhwo,io->bhwi/dot_general | solution.py:31
  59.8 4.5 %fusion.27 = f32[16,32,16,256]{3,2,1,0:T(8,128)} fusion(bf16[16,40,16,128]{3,2,1,0:T(8,128)(2,1)S(1)} %copy-done.3, bf16[16,40,4,128]{3,2,1,0:T(4,128)(2,1)S(1)} %collective-permute-done.2, bf16[3,3,256,256]{3,2,1,0:T(8,128)(2,1)S(1)} %copy-done, s32[]{:T(128)S(6)} %add.73, s32[]{:T(128)S(6)} %select_n.8), kind=kOutput, calls=%fused_computation.38 | convolution fusion | flops 541065216 | bytes 11730952 | tf_op jit(solution)/shard_map/bhwo,io->bhwi/dot_general | solution.py:31
  64.3 4.5 %fusion.48 = f32[16,32,16,256]{3,2,1,0:T(8,128)} fusion(bf16[16,40,4,128]{3,2,1,0:T(4,128)(2,1)S(1)} %collective-permute-done.2, bf16[16,40,16,128]{3,2,1,0:T(8,128)(2,1)S(1)} %copy-done.3, bf16[3,3,256,256]{3,2,1,0:T(8,128)(2,1)S(1)} %copy-done, s32[]{:T(128)S(6)} %add.74, s32[]{:T(128)S(6)} %select_n.8), kind=kOutput, calls=%fused_computation.57 | convolution fusion | flops 541065216 | bytes 11730952 | tf_op jit(solution)/shard_map/bhwo,io->bhwi/dot_general | solution.py:31
  68.8 4.5 %fusion.30 = f32[16,32,16,256]{3,2,1,0:T(8,128)} fusion(bf16[16,40,16,128]{3,2,1,0:T(8,128)(2,1)S(1)} %copy-done.3, bf16[16,40,4,128]{3,2,1,0:T(4,128)(2,1)S(1)} %collective-permute-done.2, bf16[3,3,256,256]{3,2,1,0:T(8,128)(2,1)S(1)} %copy-done, s32[]{:T(128)S(6)} %select_n.8), kind=kOutput, calls=%fused_computation.40 | convolution fusion | flops 541065216 | bytes 11730948 | tf_op jit(solution)/shard_map/bhwo,io->bhwi/dot_general | solution.py:31
  73.3 26.0 %fusion.3 = f32[16,32,16,256]{3,2,1,0:T(8,128)} fusion(f32[16,32,16,256]{3,2,1,0:T(8,128)} %fusion.8, f32[16,32,16,256]{3,2,1,0:T(8,128)} %fusion.48, f32[16,32,16,256]{3,2,1,0:T(8,128)} %fusion.21, f32[256,16,32,16]{0,3,2,1:T(8,128)} %fusion.51, f32[16,32,16,256]{3,2,1,0:T(8,128)} %fusion.27, f32[16,32,16,256]{3,2,1,0:T(8,128)} %fusion.24, ...), kind=kOutput, calls=%fused_computation.4 | convolution fusion | flops 557842432 | bytes 78839816 | tf_op jit(solution)/shard_map/bhwo,io->bhwi/dot_general | solution.py:31
  99.3 16.4 %reduce-scatter.3.cloned.1.call-done = f32[16,32,16,128]{3,2,1,0:T(8,128)} async-done(((f32[16,32,16,256]{3,2,1,0:T(8,128)}), f32[16,32,16,128]{3,2,1,0:T(8,128)}) %reduce-scatter.3.cloned.1.call-update) | async-done | bytes 4194320 | tf_op jit(solution)/shard_map/reduce_scatter | solution.py:45
  119.8 4.6 %collective-permute-start.4 = (bf16[16,2,16,128]{3,2,1,0:T(8,128)(2,1)S(1)}, bf16[16,2,16,128]{3,2,1,0:T(8,128)(2,1)S(1)}, u32[]{:S(2)}, u32[]{:S(2)}) collective-permute-start(bf16[16,2,16,128]{3,2,1,0:T(8,128)(2,1)S(1)} %get-tuple-element.12), channel_id=1, source_target_pairs={{0,8},{8,16},{16,24},{1,9},{9,17},{17,25},{2,10},{10,18},{18,26},{... | collective-permute-start | bytes 393224 | tf_op jit(solution)/shard_map/ppermute | solution.py:15
  124.4 5.3 %fusion.50 = f32[16,32,16,256]{3,2,1,0:T(8,128)} fusion(bf16[16,32,16,128]{3,2,1,0:T(8,128)(2,1)S(1)} %select_convert_fusion, bf16[3,3,256,256]{3,2,1,0:T(8,128)(2,1)} %param.6, s32[]{:T(128)S(6)} %add.73, s32[]{:T(128)S(6)} %select_n.8), kind=kOutput, calls=%fused_computation.67 | convolution fusion | flops 536870912 | bytes 10551304 | tf_op jit(solution)/shard_map/bhwo,io->bhwi/dot_general | solution.py:31
  131.7 4.6 %collective-permute-start.7 = (bf16[16,36,2,128]{3,2,1,0:T(2,128)(2,1)S(1)}, bf16[16,36,2,128]{3,2,1,0:T(2,128)(2,1)S(1)}, u32[]{:S(2)}, u32[]{:S(2)}) collective-permute-start(bf16[16,36,2,128]{3,2,1,0:T(2,128)(2,1)S(1)} %get-tuple-element.9), channel_id=1, source_target_pairs={{0,2},{2,4},{4,6},{1,3},{3,5},{5,7},{8,10},{10,12},{12,14},{9,11},... | collective-permute-start | bytes 884744 | tf_op jit(solution)/shard_map/ppermute | solution.py:15
  136.3 5.3 %fusion.12 = f32[16,32,16,256]{3,2,1,0:T(8,128)} fusion(bf16[16,2,16,128]{3,2,1,0:T(8,128)(2,1)S(1)} %collective-permute-done.5, bf16[16,32,16,128]{3,2,1,0:T(8,128)(2,1)S(1)} %select_convert_fusion, bf16[3,3,256,256]{3,2,1,0:T(8,128)(2,1)} %param.6, s32[]{:T(128)S(6)} %add.73, s32[]{:T(128)S(6)} %select_n.8), kind=kOutput, calls=%fused_computation.25 | convolution fusion | flops 541327360 | bytes 10682376 | tf_op jit(solution)/shard_map/bhwo,io->bhwi/dot_general | solution.py:31
  141.6 5.3 %fusion.16 = f32[16,32,16,256]{3,2,1,0:T(8,128)} fusion(bf16[16,32,16,128]{3,2,1,0:T(8,128)(2,1)S(1)} %select_convert_fusion, bf16[16,2,16,128]{3,2,1,0:T(8,128)(2,1)S(1)} %collective-permute-done.4, bf16[3,3,256,256]{3,2,1,0:T(8,128)(2,1)} %param.6, s32[]{:T(128)S(6)} %add.74, s32[]{:T(128)S(6)} %add.73, s32[]{:T(128)S(6)} %select_n.8), kind=kOutput, calls=%fused_computation.29 | convolution fusion | flops 541327360 | bytes 10682380 | tf_op jit(solution)/shard_map/bhwo,io->bhwi/dot_general | solution.py:31
  149.3 5.4 %fusion.38 = f32[16,32,16,256]{3,2,1,0:T(8,128)} fusion(bf16[16,36,18,128]{3,2,1,0:T(8,128)(2,1)S(1)} %get-tuple-element.7, bf16[3,3,256,256]{3,2,1,0:T(8,128)(2,1)} %param.6, s32[]{:T(128)S(6)} %add.73, s32[]{:T(128)S(6)} %add.74, s32[]{:T(128)S(6)} %select_n.8), kind=kOutput, calls=%fused_computation.45 | convolution fusion | flops 536870912 | bytes 10551308 | tf_op jit(solution)/shard_map/bhwo,io->bhwi/dot_general | solution.py:31
  154.7 5.3 %fusion.42 = f32[16,32,16,256]{3,2,1,0:T(8,128)} fusion(bf16[16,36,18,128]{3,2,1,0:T(8,128)(2,1)S(1)} %get-tuple-element.7, bf16[3,3,256,256]{3,2,1,0:T(8,128)(2,1)} %param.6, s32[]{:T(128)S(6)} %add.74, s32[]{:T(128)S(6)} %select_n.8), kind=kOutput, calls=%fused_computation.49 | convolution fusion | flops 536870912 | bytes 10551304 | tf_op jit(solution)/shard_map/bhwo,io->bhwi/dot_general | solution.py:31
  160.0 5.3 %fusion.40 = f32[16,32,16,256]{3,2,1,0:T(8,128)} fusion(bf16[16,36,18,128]{3,2,1,0:T(8,128)(2,1)S(1)} %get-tuple-element.8, bf16[3,3,256,256]{3,2,1,0:T(8,128)(2,1)} %param.6, s32[]{:T(128)S(6)} %add.73, s32[]{:T(128)S(6)} %select_n.8), kind=kOutput, calls=%fused_computation.47 | convolution fusion | flops 536870912 | bytes 10551304 | tf_op jit(solution)/shard_map/bhwo,io->bhwi/dot_general | solution.py:31
  165.3 5.3 %fusion.44 = f32[16,32,16,256]{3,2,1,0:T(8,128)} fusion(bf16[16,36,18,128]{3,2,1,0:T(8,128)(2,1)S(1)} %get-tuple-element.8, bf16[3,3,256,256]{3,2,1,0:T(8,128)(2,1)} %param.6, s32[]{:T(128)S(6)} %select_n.8), kind=kOutput, calls=%fused_computation.51 | convolution fusion | flops 536870912 | bytes 10551300 | tf_op jit(solution)/shard_map/bhwo,io->bhwi/dot_general | solution.py:31
  170.7 5.3 %fusion.36 = f32[16,32,16,256]{3,2,1,0:T(8,128)} fusion(bf16[16,36,18,128]{3,2,1,0:T(8,128)(2,1)S(1)} %get-tuple-element.8, bf16[3,3,256,256]{3,2,1,0:T(8,128)(2,1)} %param.6, s32[]{:T(128)S(6)} %add.74, s32[]{:T(128)S(6)} %select_n.8), kind=kOutput, calls=%fused_computation.43 | convolution fusion | flops 536870912 | bytes 10551304 | tf_op jit(solution)/shard_map/bhwo,io->bhwi/dot_general | solution.py:31
  176.0 25.7 %add_add_fusion = f32[16,32,16,256]{3,2,1,0:T(8,128)} fusion(f32[16,32,16,256]{3,2,1,0:T(8,128)} %fusion.16, f32[16,32,16,256]{3,2,1,0:T(8,128)} %fusion.36, f32[16,32,16,256]{3,2,1,0:T(8,128)} %fusion.38, f32[16,32,16,256]{3,2,1,0:T(8,128)} %fusion.50, f32[16,32,16,256]{3,2,1,0:T(8,128)} %fusion.40, f32[16,32,16,256]{3,2,1,0:T(8,128)} %fusion.42, ...), kind=kOutput, calls=%fused_computation.5 | convolution fusion | flops 553648128 | bytes 77660168 | tf_op jit(solution)/shard_map/bhwo,io->bhwi/dot_general | solution.py:31
  201.8 17.5 %reduce-scatter.5.cloned.1.call-done = f32[16,32,16,128]{3,2,1,0:T(8,128)} async-done(((f32[16,32,16,256]{3,2,1,0:T(8,128)}), f32[16,32,16,128]{3,2,1,0:T(8,128)}) %reduce-scatter.5.cloned.1.call-update) | async-done | bytes 4194320 | tf_op jit(solution)/shard_map/reduce_scatter | solution.py:51
  (40 shorter events, 30.8 us)
Async XLA Ops:
  6.5 25.1 %copy-start = (bf16[3,3,256,256]{3,2,1,0:T(8,128)(2,1)S(1)}, bf16[3,3,256,256]{3,2,1,0:T(8,128)(2,1)}, u32[]{:S(2)}) copy-start(bf16[3,3,256,256]{3,2,1,0:T(8,128)(2,1)} %param.7) | copy-start | bytes 3538948
  6.5 109.2 %reduce-scatter.3.cloned.1.call-start = ((), (), s32[]{:S(2)}) async-start(), calls=%async_computation.2 | async-start | bytes 12582912 | tf_op jit(solution)/shard_map/reduce_scatter | solution.py:45
  8.4 10.5 %collective-permute-start = (bf16[16,4,16,128]{3,2,1,0:T(8,128)(2,1)S(1)}, bf16[16,4,16,128]{3,2,1,0:T(8,128)(2,1)S(1)}, u32[]{:S(2)}, u32[]{:S(2)}) collective-permute-start(bf16[16,4,16,128]{3,2,1,0:T(8,128)(2,1)S(1)} %get-tuple-element.14), channel_id=1, source_target_pairs={{0,8},{8,16},{16,24},{1,9},{9,17},{17,25},{2,10},{10,18},{18,26},{... | collective-permute-start | bytes 786440 | tf_op jit(solution)/shard_map/ppermute | solution.py:15
  13.3 10.0 %collective-permute-start.1 = (bf16[16,4,16,128]{3,2,1,0:T(8,128)(2,1)}, bf16[16,4,16,128]{3,2,1,0:T(8,128)(2,1)}, u32[]{:S(2)}, u32[]{:S(2)}) collective-permute-start(bf16[16,4,16,128]{3,2,1,0:T(8,128)(2,1)} %get-tuple-element.13), channel_id=1, source_target_pairs={{8,0},{16,8},{24,16},{9,1},{17,9},{25,17},{10,2},{18,10},{26,18},{... | collective-permute-start | bytes 786440 | tf_op jit(solution)/shard_map/ppermute | solution.py:17
  18.9 12.7 %copy-start.4 = (bf16[16,32,16,128]{3,2,1,0:T(8,128)(2,1)S(1)}, bf16[16,32,16,128]{3,2,1,0:T(8,128)(2,1)}, u32[]{:S(2)}) copy-start(bf16[16,32,16,128]{3,2,1,0:T(8,128)(2,1)} %param.4) | copy-start | bytes 6291460
  24.3 1.5 copy-start.2
  27.4 20.1 %collective-permute-start.3 = (bf16[16,40,4,128]{3,2,1,0:T(4,128)(2,1)}, bf16[16,40,4,128]{3,2,1,0:T(4,128)(2,1)}, u32[]{:S(2)}, u32[]{:S(2)}) collective-permute-start(bf16[16,40,4,128]{3,2,1,0:T(4,128)(2,1)} %get-tuple-element.5), channel_id=1, source_target_pairs={{0,2},{2,4},{4,6},{1,3},{3,5},{5,7},{8,10},{10,12},{12,14},{9,11},... | collective-permute-start | bytes 1966088 | tf_op jit(solution)/shard_map/ppermute | solution.py:15
  36.1 23.7 %collective-permute-start.2 = (bf16[16,40,4,128]{3,2,1,0:T(4,128)(2,1)}, bf16[16,40,4,128]{3,2,1,0:T(4,128)(2,1)S(1)}, u32[]{:S(2)}, u32[]{:S(2)}) collective-permute-start(bf16[16,40,4,128]{3,2,1,0:T(4,128)(2,1)} %get-tuple-element.6), channel_id=1, source_target_pairs={{2,0},{4,2},{6,4},{3,1},{5,3},{7,5},{10,8},{12,10},{14,12},{11,9},... | collective-permute-start | bytes 1966088 | tf_op jit(solution)/shard_map/ppermute | solution.py:17
  43.0 4.5 %copy-start.3 = (bf16[16,40,16,128]{3,2,1,0:T(8,128)(2,1)S(1)}, bf16[16,40,16,128]{3,2,1,0:T(8,128)(2,1)}, u32[]{:S(2)}) copy-start(bf16[16,40,16,128]{3,2,1,0:T(8,128)(2,1)} %copy-done.2) | copy-start | bytes 7864324
  99.2 16.5 %copy-start.6 = (bf16[16,32,16,128]{3,2,1,0:T(8,128)(2,1)S(1)}, bf16[16,32,16,128]{3,2,1,0:T(8,128)(2,1)}, u32[]{:S(2)}) copy-start(bf16[16,32,16,128]{3,2,1,0:T(8,128)(2,1)} %param.5) | copy-start | bytes 6291460
  99.3 120.0 %reduce-scatter.5.cloned.1.call-start = ((), (), s32[]{:S(2)}) async-start(), calls=%async_computation.3 | async-start | bytes 12582912 | tf_op jit(solution)/shard_map/reduce_scatter | solution.py:51
  118.5 11.2 %collective-permute-start.5 = (bf16[16,2,16,128]{3,2,1,0:T(8,128)(2,1)S(1)}, bf16[16,2,16,128]{3,2,1,0:T(8,128)(2,1)S(1)}, u32[]{:S(2)}, u32[]{:S(2)}) collective-permute-start(bf16[16,2,16,128]{3,2,1,0:T(8,128)(2,1)S(1)} %get-tuple-element.11), channel_id=1, source_target_pairs={{8,0},{16,8},{24,16},{9,1},{17,9},{25,17},{10,2},{18,10},{26,18},{... | collective-permute-start | bytes 393224 | tf_op jit(solution)/shard_map/ppermute | solution.py:17
  119.8 9.9 %collective-permute-start.4 = (bf16[16,2,16,128]{3,2,1,0:T(8,128)(2,1)S(1)}, bf16[16,2,16,128]{3,2,1,0:T(8,128)(2,1)S(1)}, u32[]{:S(2)}, u32[]{:S(2)}) collective-permute-start(bf16[16,2,16,128]{3,2,1,0:T(8,128)(2,1)S(1)} %get-tuple-element.12), channel_id=1, source_target_pairs={{0,8},{8,16},{16,24},{1,9},{9,17},{17,25},{2,10},{10,18},{18,26},{... | collective-permute-start | bytes 393224 | tf_op jit(solution)/shard_map/ppermute | solution.py:15
  130.2 16.7 %collective-permute-start.6 = (bf16[16,36,2,128]{3,2,1,0:T(2,128)(2,1)S(1)}, bf16[16,36,2,128]{3,2,1,0:T(2,128)(2,1)S(1)}, u32[]{:S(2)}, u32[]{:S(2)}) collective-permute-start(bf16[16,36,2,128]{3,2,1,0:T(2,128)(2,1)S(1)} %get-tuple-element.10), channel_id=1, source_target_pairs={{2,0},{4,2},{6,4},{3,1},{5,3},{7,5},{10,8},{12,10},{14,12},{11,9},... | collective-permute-start | bytes 884744 | tf_op jit(solution)/shard_map/ppermute | solution.py:17
  131.7 15.2 %collective-permute-start.7 = (bf16[16,36,2,128]{3,2,1,0:T(2,128)(2,1)S(1)}, bf16[16,36,2,128]{3,2,1,0:T(2,128)(2,1)S(1)}, u32[]{:S(2)}, u32[]{:S(2)}) collective-permute-start(bf16[16,36,2,128]{3,2,1,0:T(2,128)(2,1)S(1)} %get-tuple-element.9), channel_id=1, source_target_pairs={{0,2},{2,4},{4,6},{1,3},{3,5},{5,7},{8,10},{10,12},{12,14},{9,11},... | collective-permute-start | bytes 884744 | tf_op jit(solution)/shard_map/ppermute | solution.py:15
  149.2 5.4 %copy-start.5 = (bf16[16,36,18,128]{3,2,1,0:T(8,128)(2,1)}, bf16[16,36,18,128]{3,2,1,0:T(8,128)(2,1)S(1)}, u32[]{:S(2)}) copy-start(bf16[16,36,18,128]{3,2,1,0:T(8,128)(2,1)S(1)} %get-tuple-element.7) | copy-start | bytes 7962628
  201.7 21.4 %copy-start.1 = (bf16[3,3,256,256]{3,2,1,0:T(8,128)(2,1)S(1)}, bf16[3,3,256,256]{3,2,1,0:T(8,128)(2,1)}, u32[]{:S(2)}) copy-start(bf16[3,3,256,256]{3,2,1,0:T(8,128)(2,1)} %param.7) | copy-start | bytes 3538948
Sparse Core Ops, SparseCore 0:
  99.4 16.2 reduce-scatter.2
  201.9 17.3 reduce-scatter.4
where the time goes:
time: 231 us; the launch traced here: 230 us
  matrix products  133 us (58%)
  waiting for transfers between devices  41.4 us (18%)
  starting transfers between devices  23.9 us (10%)
  between operations  13.6 us (6%)
  other arithmetic  9.38 us (4%)
  local copies, waits for them, and re-layouts  8.31 us (4%)
    dot_general x18, matrix products, tap_sum(): jnp.einsum('bhwo,io->bhwi', piece, weight[tap_row, tap_col], preferred_el...  133 us
    ppermute x4, starting transfers between devices, padded_2(): lax.ppermute(tail, axis, [(i, (i + 1) % count) for i in range(ends)])  18.3 us
    reduce_scatter x1, waiting for transfers between devices, per_device(): lax.psum_scatter(tap_sum(inner, cols_one, 2, rows, cols), 'filt', scatter...  17.5 us
    reduce_scatter x1, waiting for transfers between devices, per_device(): lax.psum_scatter(tap_sum(outer, cols_two, 4, rows, cols), 'filt', scatter...  16.4 us
    ppermute x4, starting transfers between devices, padded_2(): lax.ppermute(head, axis, [((i + 1) % count, i) for i in range(ends)])  5.56 us
  transfers between devices with their start and end apart: 10, of which 5 were waited for; matrix products, arithmetic and copies ran while one was open for 19% of the time, Pallas kernels for 0%

commit v1 on v0

v1 whole, which is shorter than its diff:
```python
import functools

import jax
import jax.numpy as jnp
from jax import lax
from jax.experimental import pallas as pl
from jax.experimental.pallas import tpu as pltpu
from jax.sharding import PartitionSpec as P

MESH = pl.DeviceIdType.MESH
GS = 4
HS = 2


def conv(buf, weight, row, col, rows, cols, spacing):
    batch = buf.shape[3]
    pieces = []
    for p in range(3):
        for q in range(3):
            for half in range(2):
                piece = buf[half, pl.ds(row + spacing * (2 - p), rows), pl.ds(col + spacing * (2 - q), cols)]
                pieces.append(piece.reshape(rows * cols * batch, piece.shape[-1]))
    return jnp.dot(jnp.concatenate(pieces, axis=1), weight[...], preferred_element_type=jnp.float32)


def kernel(nrow, ncol, g_in, p_in, w1, w2, out, gbuf, pbuf, hbuf, obuf, send, recv, local):
    r, c, f = lax.axis_index("row"), lax.axis_index("col"), lax.axis_index("filt")
    o = 1 - f
    rows = g_in.shape[0] // 2
    cols = g_in.shape[1]
    batch, chan = g_in.shape[2], g_in.shape[3]
    has_left, has_right = c > 0, c < ncol - 1
    has_top, has_bot = r > 0, r < nrow - 1
    first, last = jnp.logical_and(f == 0, r == 0), jnp.logical_and(f == 1, r == nrow - 1)
    has_up, has_down = jnp.logical_not(first), jnp.logical_not(last)
    up = (r - o, c, o)
    down = (r + f, c, o)
    partner = (r, c, o)

    @pl.when(first)
    def _():
        gbuf[:, :GS] = jnp.zeros((2, GS) + gbuf.shape[2:], gbuf.dtype)
        hbuf[:, :HS] = jnp.zeros((2, HS) + hbuf.shape[2:], hbuf.dtype)

    @pl.when(last)
    def _():
        gbuf[:, rows + GS:] = jnp.zeros((2, GS) + gbuf.shape[2:], gbuf.dtype)
        hbuf[:, rows + HS:] = jnp.zeros((2, HS) + hbuf.shape[2:], hbuf.dtype)

    @pl.when(jnp.logical_not(has_left))
    def _():
        gbuf[:, :, :GS] = jnp.zeros((2, rows + 2 * GS, GS, batch, chan), gbuf.dtype)
        hbuf[:, :, :HS] = jnp.zeros((2, rows + 2 * HS, HS, batch, chan), hbuf.dtype)

    @pl.when(jnp.logical_not(has_right))
    def _():
        gbuf[:, :, cols + GS:] = jnp.zeros((2, rows + 2 * GS, GS, batch, chan), gbuf.dtype)
        hbuf[:, :, cols + HS:] = jnp.zeros((2, rows + 2 * HS, HS, batch, chan), hbuf.dtype)

    barrier = pltpu.get_barrier_semaphore()
    pl.semaphore_signal(barrier, inc=1, device_id=partner, device_id_type=MESH)
    count = jnp.int32(1)
    for there, rr, cc in ((has_left, r, c - 1), (has_right, r, c + 1), (has_top, r - 1, c), (has_bot, r + 1, c)):
        @pl.when(there)
        def _(rr=rr, cc=cc):
            for ff in range(2):
                pl.semaphore_signal(barrier, inc=1, device_id=(rr, cc, ff), device_id_type=MESH)
        count = count + jnp.where(there, 2, 0)
    pl.semaphore_wait(barrier, count)

    def copy(src, dst, sidx, ridx, device):
        return pltpu.make_async_remote_copy(
            src_ref=src, dst_ref=dst, send_sem=send.at[sidx], recv_sem=recv.at[ridx],
            device_id=device, device_id_type=MESH)

    def landed(dst, ridx):
        copy(dst, dst, 0, ridx, partner).wait_recv()

    sends = []

    def start(there, src, dst, ridx, device):
        sidx = len(sends)
        what = copy(src, dst, sidx, ridx, device)
        sends.append((there, what))
        if there is None:
            what.start()
        else:
            @pl.when(there)
            def _():
                what.start()

    grow, gcol = pl.ds(GS, rows), pl.ds(GS, cols)
    hrow, hcol = pl.ds(HS, rows), pl.ds(HS, cols)
    L, R, T, B, MAIN, PRE, CORNER, HL, HR, HT, HB, HCORNER, OUT = 0, 2, 4, 6, 8, 9, 10, 14, 15, 16, 17, 18, 22

    for ff in range(2):
        start(has_right, g_in.at[pl.ds(rows * ff, rows), pl.ds(cols - GS, GS)], gbuf.at[f, grow, pl.ds(0, GS)],
              L + f, (r, c + 1, ff))
        start(has_left, g_in.at[pl.ds(rows * ff, rows), pl.ds(0, GS)], gbuf.at[f, grow, pl.ds(cols + GS, GS)],
              R + f, (r, c - 1, ff))
    span = rows + GS
    start(None, g_in.at[pl.ds((rows - GS) * o, span)], gbuf.at[f, pl.ds(GS * f, span), gcol], MAIN, partner)
    mine = pltpu.make_async_copy(
        g_in.at[pl.ds((rows - GS) * f, span)], gbuf.at[f, pl.ds(GS * o, span), gcol], local.at[0])
    mine.start()
    start(has_bot, g_in.at[pl.ds(2 * rows - GS, GS)], gbuf.at[f, pl.ds(0, GS), gcol], T + f, (r + 1, c, 0))
    start(has_top, g_in.at[pl.ds(0, GS)], gbuf.at[f, pl.ds(rows + GS, GS), gcol], B + f, (r - 1, c, 1))
    start(None, p_in.at[pl.ds(rows * o, rows)], pbuf.at[f], PRE, partner)
    own_pre = pltpu.make_async_copy(p_in.at[pl.ds(rows * f, rows)], pbuf.at[f], local.at[1])
    own_pre.start()

    landed(gbuf.at[o, pl.ds(GS * o, span), gcol], MAIN)
    mine.wait()
    landed(pbuf.at[o], PRE)
    own_pre.wait()

    @pl.when(jnp.logical_and(f == 0, has_top))
    def _():
        for half in range(2):
            landed(gbuf.at[half, pl.ds(0, GS), gcol], T + half)

    @pl.when(jnp.logical_and(f == 1, has_bot))
    def _():
        for half in range(2):
            landed(gbuf.at[half, pl.ds(rows + GS, GS), gcol], B + half)

    def hidden(row, col, nr, nc):
        total = conv(gbuf, w2, row, col, nr, nc, GS)
        for half in range(2):
            keep = pbuf[half, pl.ds(row, nr), pl.ds(col, nc)].reshape(nr * nc * batch, chan).astype(jnp.float32) > 0
            part = jnp.where(keep, total[:, half * chan:(half + 1) * chan], 0.0).astype(hbuf.dtype)
            hbuf[half, pl.ds(row + HS, nr), pl.ds(col + HS, nc)] = part.reshape(nr, nc, batch, chan)

    @pl.loop(0, rows // 4)
    def _(i):
        hidden(i * 4, GS, 4, cols - 2 * GS)

    @pl.when(has_left)
    def _():
        for half in range(2):
            landed(gbuf.at[half, grow, pl.ds(0, GS)], L + half)

    @pl.when(has_right)
    def _():
        for half in range(2):
            landed(gbuf.at[half, grow, pl.ds(cols + GS, GS)], R + half)

    both = pl.ds(0, 2)

    def corners(buf, width, size, base):
        for side, there, col in ((0, has_left, 0), (1, has_right, cols + width)):
            at = pl.ds(col, width)
            start(jnp.logical_and(there, has_up), buf.at[both, pl.ds(width, width), at],
                  buf.at[both, pl.ds(rows + width, width), at], base + side, up)
            start(jnp.logical_and(there, has_down), buf.at[both, pl.ds(rows, width), at],
                  buf.at[both, pl.ds(0, width), at], base + 2 + side, down)

    def corners_landed(buf, width, base):
        for side, there, col in ((0, has_left, 0), (1, has_right, cols + width)):
            at = pl.ds(col, width)

            @pl.when(jnp.logical_and(there, has_down))
            def _(side=side, at=at):
                landed(buf.at[both, pl.ds(rows + width, width), at], base + side)

            @pl.when(jnp.logical_and(there, has_up))
            def _(side=side, at=at):
                landed(buf.at[both, pl.ds(0, width), at], base + 2 + side)

    corners(gbuf, GS, GS, CORNER)

    @pl.loop(1, rows // 4 - 1)
    def _(i):
        hidden(i * 4, 0, 4, GS)
        hidden(i * 4, cols - GS, 4, GS)

    corners_landed(gbuf, GS, CORNER)

    @pl.loop(0, 2)
    def _(i):
        at = i * (rows - 4)
        hidden(at, 0, 4, GS)
        hidden(at, cols - GS, 4, GS)

    start(has_right, hbuf.at[both, hrow, pl.ds(cols, HS)], hbuf.at[both, hrow, pl.ds(0, HS)], HL, (r, c + 1, f))
    start(has_left, hbuf.at[both, hrow, pl.ds(HS, HS)], hbuf.at[both, hrow, pl.ds(cols + HS, HS)], HR, (r, c - 1, f))
    start(has_up, hbuf.at[both, pl.ds(HS, HS), hcol], hbuf.at[both, pl.ds(rows + HS, HS), hcol], HB, up)
    start(has_down, hbuf.at[both, pl.ds(rows, HS), hcol], hbuf.at[both, pl.ds(0, HS), hcol], HT, down)

    def result(row, col, nr, nc):
        total = conv(hbuf, w1, row, col, nr, nc, HS)
        for half in range(2):
            part = total[:, half * chan:(half + 1) * chan].astype(obuf.dtype)
            obuf[half, pl.ds(row, nr), pl.ds(col, nc)] = part.reshape(nr, nc, batch, chan)

    @pl.loop(0, (rows - 2 * HS) // 4)
    def _(i):
        result(HS + i * 4, HS, 4, cols - 2 * HS)

    @pl.when(has_up)
    def _():
        landed(hbuf.at[both, pl.ds(0, HS), hcol], HT)

    @pl.when(has_down)
    def _():
        landed(hbuf.at[both, pl.ds(rows + HS, HS), hcol], HB)

    @pl.loop(0, 2)
    def _(i):
        result(i * (rows - HS), HS, HS, cols - 2 * HS)

    @pl.when(has_left)
    def _():
        landed(hbuf.at[both, hrow, pl.ds(0, HS)], HL)

    @pl.when(has_right)
    def _():
        landed(hbuf.at[both, hrow, pl.ds(cols + HS, HS)], HR)

    corners(hbuf, HS, HS, HCORNER)

    @pl.loop(0, 2)
    def _(i):
        result(HS, i * (cols - HS), rows - 2 * HS, HS)

    corners_landed(hbuf, HS, HCORNER)

    @pl.loop(0, 2)
    def _(i):
        result(i * (rows - HS), 0, HS, HS)
        result(i * (rows - HS), cols - HS, HS, HS)

    start(None, obuf.at[o], out.at[pl.ds(rows * f, rows)], OUT, partner)
    keep = pltpu.make_async_copy(obuf.at[f], out.at[pl.ds(rows * f, rows)], local.at[2])
    keep.start()
    landed(out.at[pl.ds(rows * o, rows)], OUT)
    keep.wait()
    for there, what in sends:
        if there is None:
            what.wait_send()
        else:
            @pl.when(there)
            def _(what=what):
                what.wait_send()


def solution(mesh):
    nrow, ncol = mesh.shape["row"], mesh.shape["col"]

    def per_device(grad_out, pre_act, weight_one, weight_two):
        batch, rows, cols, chan = grad_out.shape
        taps = lambda w: jnp.swapaxes(w, 2, 3).reshape(-1, w.shape[2])
        inward = lambda a: jnp.transpose(a, (1, 2, 0, 3))
        strip = rows // 2
        kind = grad_out.dtype
        out = pl.pallas_call(
            functools.partial(kernel, nrow, ncol),
            out_shape=jax.ShapeDtypeStruct((rows, cols, batch, chan), kind),
            in_specs=[pl.BlockSpec(memory_space=pl.ANY)] * 2 + [pl.BlockSpec(memory_space=pltpu.VMEM)] * 2,
            out_specs=pl.BlockSpec(memory_space=pl.ANY),
            scratch_shapes=[
                pltpu.VMEM((2, strip + 2 * GS, cols + 2 * GS, batch, chan), kind),
                pltpu.VMEM((2, strip, cols, batch, chan), kind),
                pltpu.VMEM((2, strip + 2 * HS, cols + 2 * HS, batch, chan), kind),
                pltpu.VMEM((2, strip, cols, batch, chan), kind),
                pltpu.SemaphoreType.DMA((24,)),
                pltpu.SemaphoreType.DMA((23,)),
                pltpu.SemaphoreType.DMA((3,)),
            ],
            compiler_params=pltpu.CompilerParams(
                collective_id=0, has_side_effects=True, vmem_limit_bytes=48 * 1024 * 1024),
            cost_estimate=pl.CostEstimate(
                flops=4 * 9 * batch * rows * cols * chan * 2 * chan, bytes_accessed=8 * batch * rows * cols * chan,
                transcendentals=0),
        )(inward(grad_out), inward(pre_act), taps(weight_one), taps(weight_two))
        return jnp.transpose(out, (2, 0, 1, 3))

    placed = (P(None, "row", "col", "filt"), P(None, "row", "col", "filt"), P(), P())
    return jax.shard_map(
        per_device, mesh=mesh, in_specs=placed, out_specs=P(None, "row", "col", "filt"), check_vma=False)
```

time: 231 us -> 65.3 us (0.28)
  matrix products: 133 us -> 0 us
  Pallas kernels: 0 us -> 51.7 us
  waiting for transfers between devices: 41.4 us -> 0 us
  starting transfers between devices: 23.9 us -> 0 us
  between operations: 13.6 us -> 0.03 us
  other arithmetic: 9.38 us -> 0 us
  local copies, waits for them, and re-layouts: 8.31 us -> 13.4 us
    dot_general x18 -> x0, matrix products: 133 us -> none  [tap_sum(): jnp.einsum('bhwo,io->bhwi', piece, weight[tap_row, tap_col], preferred_el...]
    pallas_call x0 -> x1, Pallas kernels: none -> 51.7 us  [per_device(): pl.pallas_call(functools.partial(kernel, nrow, ncol), out_shape=jax.Shape...]
    reduce_scatter x2 -> x0, waiting for transfers between devices: 33.9 us -> none  [the longest x1 17.5 us: per_device(): lax.psum_scatter(tap_sum(inner, cols_one, 2, rows, cols), 'filt', scatter...]
    ppermute x8 -> x0, starting transfers between devices: 23.8 us -> none  [the longest x4 18.3 us: padded_2(): lax.ppermute(tail, axis, [(i, (i + 1) % count) for i in range(ends)])]
    transpose x0 -> x4, local copies, waits for them, and re-layouts: none -> 13.4 us  [the longest x1 9.11 us: per_device(): inward = lambda a: jnp.transpose(a, (1, 2, 0, 3))]
    ppermute x8 -> x0, waiting for transfers between devices: 7.44 us -> none  [the longest x4 4.23 us: padded_2(): lax.ppermute(tail, axis, [(i, (i + 1) % count) for i in range(ends)])]
    convert_element_type x2 -> x0, other arithmetic: 6.62 us -> none  [the longest x1 3.84 us: per_device(): return grad_in.astype(jnp.bfloat16)]
    unnamed x16 -> x2, local copies, waits for them, and re-layouts: 3.88 us -> 0.01 us
  transfers between devices with their start and end apart: 10 -> 0, of which waited for: 5 -> 0; matrix products, arithmetic and copies ran while one was open for 19% -> 0% of each run, Pallas kernels for 0% -> 0%
where the time goes in v1:
time: 65.3 us; the launch traced here: 65.1 us
  Pallas kernels  51.7 us (79%)
  local copies, waits for them, and re-layouts  13.4 us (21%)
    pallas_call x1, Pallas kernels, per_device(): pl.pallas_call(functools.partial(kernel, nrow, ncol), out_shape=jax.Shape...  51.7 us
    transpose x1, local copies, waits for them, and re-layouts, per_device(): inward = lambda a: jnp.transpose(a, (1, 2, 0, 3))  9.11 us
    transpose x2, local copies, waits for them, and re-layouts, per_device(): taps = lambda w: jnp.swapaxes(w, 2, 3).reshape(-1, w.shape[2])  2.39 us
    transpose x1, local copies, waits for them, and re-layouts, per_device(): return jnp.transpose(out, (2, 0, 1, 3))  1.86 us

profile of v1, /device:TPU:0, one launch (start us, length us, event | category | flops | bytes accessed | tf_op | source)
XLA Modules:
  0.0 65.1 jit_solution(11759795342399882640)
XLA Ops:
  0.0 0.0 copy-start
  0.0 1.7 %copy.7 = bf16[3,3,256,256]{3,2,1,0:T(8,128)(2,1)S(1)} copy(bf16[3,3,256,256]{2,3,1,0:T(8,128)(2,1)} %bitcast.12) | data formatting | bytes 2359296 | tf_op jit(solution)/shard_map/transpose | solution.py:252
  1.7 0.0 copy-done
  1.7 0.7 %copy.8 = bf16[3,3,256,256]{3,2,1,0:T(8,128)(2,1)S(1)} copy(bf16[3,3,256,256]{2,3,1,0:T(8,128)(2,1)S(1)} %bitcast.13) | data formatting | bytes 2359296 | tf_op jit(solution)/shard_map/transpose | solution.py:252
  2.4 9.1 %copy_bitcast_fusion = (bf16[32,16,16,128]{3,2,1,0:T(8,128)(2,1)}, bf16[32,16,16,128]{3,2,1,0:T(8,128)(2,1)}) fusion(bf16[16,32,16,128]{3,2,1,0:T(8,128)(2,1)} %param.5, bf16[16,32,16,128]{3,2,1,0:T(8,128)(2,1)} %param.4), kind=kLoop, calls=%fused_computation | loop fusion | bytes 8388608 | tf_op jit(solution)/shard_map/transpose | solution.py:253
  11.5 51.7 %shard_map.46 = bf16[32,16,16,128]{3,2,1,0:T(8,128)(2,1)S(1)} custom-call(bf16[32,16,16,128]{3,2,1,0:T(8,128)(2,1)} %get-tuple-element.6.g_in, bf16[32,16,16,128]{3,2,1,0:T(8,128)(2,1)} %get-tuple-element.5.p_in, bf16[2304,256]{1,0:T(8,128)(2,1)S(1)} %bitcast.10, bf16[2304,256]{1,0:T(8,128)(2,1)S(1)} %bitcast.11), custom_call_target="tpu_custom_call" | custom-call | flops 9663676416 | bytes 8388608 | tf_op jit(solution)/shard_map/pallas_call | solution.py:256
  63.3 1.9 %copy.9 = bf16[16,32,16,128]{3,2,1,0:T(8,128)(2,1)} copy(bf16[16,32,16,128]{3,0,2,1:T(8,128)(2,1)S(1)} %bitcast.9) | data formatting | bytes 4194304 | tf_op jit(solution)/shard_map/transpose | solution.py:276
Async XLA Ops:
  0.0 1.7 %copy-start = (bf16[3,3,256,256]{3,2,1,0:T(8,128)(2,1)S(1)}, bf16[3,3,256,256]{3,2,1,0:T(8,128)(2,1)}, u32[]{:S(2)}) copy-start(bf16[3,3,256,256]{3,2,1,0:T(8,128)(2,1)} %param.7) | copy-start | bytes 3538948

commit v2 on v1

--- a/solution.py
+++ b/solution.py
@@ -23,7 +23,7 @@
     return jnp.dot(jnp.concatenate(pieces, axis=1), weight[...], preferred_element_type=jnp.float32)
 
 
-def kernel(nrow, ncol, g_in, p_in, w1, w2, out, gbuf, pbuf, hbuf, obuf, send, recv, local):
+def kernel(nrow, ncol, g_in, p_in, w1, w2, out, gbuf, pbuf, hbuf, obuf, gvia, hvia, send, recv, local):
     r, c, f = lax.axis_index("row"), lax.axis_index("col"), lax.axis_index("filt")
     o = 1 - f
     rows = g_in.shape[0] // 2
@@ -36,6 +36,8 @@
     up = (r - o, c, o)
     down = (r + f, c, o)
     partner = (r, c, o)
+    folded = ncol == 4
+    across = lax.rem(c + 2, 4)
 
     @pl.when(first)
     def _():
@@ -66,6 +68,9 @@
             for ff in range(2):
                 pl.semaphore_signal(barrier, inc=1, device_id=(rr, cc, ff), device_id_type=MESH)
         count = count + jnp.where(there, 2, 0)
+    if folded:
+        pl.semaphore_signal(barrier, inc=1, device_id=(r, across, f), device_id_type=MESH)
+        count = count + 1
     pl.semaphore_wait(barrier, count)
 
     def copy(src, dst, sidx, ridx, device):
@@ -91,12 +96,20 @@
 
     grow, gcol = pl.ds(GS, rows), pl.ds(GS, cols)
     hrow, hcol = pl.ds(HS, rows), pl.ds(HS, cols)
-    L, R, T, B, MAIN, PRE, CORNER, HL, HR, HT, HB, HCORNER, OUT = 0, 2, 4, 6, 8, 9, 10, 14, 15, 16, 17, 18, 22
-
+    L, R, T, B, MAIN, PRE, CORNER, HL, HR, HT, HB, HCORNER, OUT, VIA, HVIA = (
+        0, 2, 4, 6, 8, 9, 10, 14, 15, 16, 17, 18, 22, 23, 24)
+
+    if folded:
+        start(c == 1, g_in.at[pl.ds(rows, rows), pl.ds(cols - GS, GS)], gvia, VIA, (r, across, f))
+        start(c == 2, g_in.at[pl.ds(rows, rows), pl.ds(0, GS)], gvia, VIA, (r, across, f))
     for ff in range(2):
-        start(has_right, g_in.at[pl.ds(rows * ff, rows), pl.ds(cols - GS, GS)], gbuf.at[f, grow, pl.ds(0, GS)],
+        to_right, to_left = has_right, has_left
+        if folded and ff == 1:
+            to_right = jnp.logical_and(has_right, c != 1)
+            to_left = jnp.logical_and(has_left, c != 2)
+        start(to_right, g_in.at[pl.ds(rows * ff, rows), pl.ds(cols - GS, GS)], gbuf.at[f, grow, pl.ds(0, GS)],
               L + f, (r, c + 1, ff))
-        start(has_left, g_in.at[pl.ds(rows * ff, rows), pl.ds(0, GS)], gbuf.at[f, grow, pl.ds(cols + GS, GS)],
+        start(to_left, g_in.at[pl.ds(rows * ff, rows), pl.ds(0, GS)], gbuf.at[f, grow, pl.ds(cols + GS, GS)],
               R + f, (r, c - 1, ff))
     span = rows + GS
     start(None, g_in.at[pl.ds((rows - GS) * o, span)], gbuf.at[f, pl.ds(GS * f, span), gcol], MAIN, partner)
@@ -109,6 +122,13 @@
     own_pre = pltpu.make_async_copy(p_in.at[pl.ds(rows * f, rows)], pbuf.at[f], local.at[1])
     own_pre.start()
 
+    if folded:
+        @pl.when(jnp.logical_or(c == 0, c == 3))
+        def _():
+            landed(gvia, VIA)
+        start(c == 3, gvia, gbuf.at[f, grow, pl.ds(0, GS)], L + f, (r, c - 1, 1))
+        start(c == 0, gvia, gbuf.at[f, grow, pl.ds(cols + GS, GS)], R + f, (r, c + 1, 1))
+
     landed(gbuf.at[o, pl.ds(GS * o, span), gcol], MAIN)
     mine.wait()
     landed(pbuf.at[o], PRE)
@@ -182,8 +202,14 @@
         hidden(at, 0, 4, GS)
         hidden(at, cols - GS, 4, GS)
 
-    start(has_right, hbuf.at[both, hrow, pl.ds(cols, HS)], hbuf.at[both, hrow, pl.ds(0, HS)], HL, (r, c + 1, f))
-    start(has_left, hbuf.at[both, hrow, pl.ds(HS, HS)], hbuf.at[both, hrow, pl.ds(cols + HS, HS)], HR, (r, c - 1, f))
+    to_right, to_left = has_right, has_left
+    if folded:
+        start(jnp.logical_and(c == 1, f == 1), hbuf.at[both, hrow, pl.ds(cols, HS)], hvia, HVIA, (r, across, f))
+        start(jnp.logical_and(c == 2, f == 1), hbuf.at[both, hrow, pl.ds(HS, HS)], hvia, HVIA, (r, across, f))
+        to_right = jnp.logical_and(has_right, jnp.logical_or(c != 1, f == 0))
+        to_left = jnp.logical_and(has_left, jnp.logical_or(c != 2, f == 0))
+    start(to_right, hbuf.at[both, hrow, pl.ds(cols, HS)], hbuf.at[both, hrow, pl.ds(0, HS)], HL, (r, c + 1, f))
+    start(to_left, hbuf.at[both, hrow, pl.ds(HS, HS)], hbuf.at[both, hrow, pl.ds(cols + HS, HS)], HR, (r, c - 1, f))
     start(has_up, hbuf.at[both, pl.ds(HS, HS), hcol], hbuf.at[both, pl.ds(rows + HS, HS), hcol], HB, up)
     start(has_down, hbuf.at[both, pl.ds(rows, HS), hcol], hbuf.at[both, pl.ds(0, HS), hcol], HT, down)
 
@@ -196,6 +222,13 @@
     @pl.loop(0, (rows - 2 * HS) // 4)
     def _(i):
         result(HS + i * 4, HS, 4, cols - 2 * HS)
+
+    if folded:
+        @pl.when(jnp.logical_and(jnp.logical_or(c == 0, c == 3), f == 1))
+        def _():
+            landed(hvia, HVIA)
+        start(jnp.logical_and(c == 3, f == 1), hvia, hbuf.at[both, hrow, pl.ds(0, HS)], HL, (r, c - 1, f))
+        start(jnp.logical_and(c == 0, f == 1), hvia, hbuf.at[both, hrow, pl.ds(cols + HS, HS)], HR, (r, c + 1, f))
 
     @pl.when(has_up)
     def _():
@@ -263,8 +296,10 @@
                 pltpu.VMEM((2, strip, cols, batch, chan), kind),
                 pltpu.VMEM((2, strip + 2 * HS, cols + 2 * HS, batch, chan), kind),
                 pltpu.VMEM((2, strip, cols, batch, chan), kind),
-                pltpu.SemaphoreType.DMA((24,)),
-                pltpu.SemaphoreType.DMA((23,)),
+                pltpu.VMEM((strip, GS, batch, chan), kind),
+                pltpu.VMEM((2, strip, HS, batch, chan), kind),
+                pltpu.SemaphoreType.DMA((30,)),
+                pltpu.SemaphoreType.DMA((25,)),
                 pltpu.SemaphoreType.DMA((3,)),
             ],
             compiler_params=pltpu.CompilerParams(

time: 65.3 us -> 56.6 us (0.87)
  Pallas kernels: 51.7 us -> 43 us
    pallas_call x1, Pallas kernels: 51.7 us -> 43 us  [per_device(): pl.pallas_call(functools.partial(kernel, nrow, ncol), out_shape=jax.Shape...]
where the time goes in v2:
time: 56.6 us; the launch traced here: 56.4 us
  Pallas kernels  43 us (76%)
  local copies, waits for them, and re-layouts  13.4 us (24%)
    pallas_call x1, Pallas kernels, per_device(): pl.pallas_call(functools.partial(kernel, nrow, ncol), out_shape=jax.Shape...  43 us
    transpose x1, local copies, waits for them, and re-layouts, per_device(): inward = lambda a: jnp.transpose(a, (1, 2, 0, 3))  9.11 us
    transpose x2, local copies, waits for them, and re-layouts, per_device(): taps = lambda w: jnp.swapaxes(w, 2, 3).reshape(-1, w.shape[2])  2.39 us
    transpose x1, local copies, waits for them, and re-layouts, per_device(): return jnp.transpose(out, (2, 0, 1, 3))  1.86 us

profile of v2, /device:TPU:0, one launch (start us, length us, event | category | flops | bytes accessed | tf_op | source)
XLA Modules:
  0.0 56.4 jit_solution(3487662611643341873)
XLA Ops:
  0.0 0.0 copy-start
  0.0 1.7 %copy.7 = bf16[3,3,256,256]{3,2,1,0:T(8,128)(2,1)S(1)} copy(bf16[3,3,256,256]{2,3,1,0:T(8,128)(2,1)} %bitcast.12) | data formatting | bytes 2359296 | tf_op jit(solution)/shard_map/transpose | solution.py:285
  1.7 0.0 copy-done
  1.7 0.7 %copy.8 = bf16[3,3,256,256]{3,2,1,0:T(8,128)(2,1)S(1)} copy(bf16[3,3,256,256]{2,3,1,0:T(8,128)(2,1)S(1)} %bitcast.13) | data formatting | bytes 2359296 | tf_op jit(solution)/shard_map/transpose | solution.py:285
  2.4 9.1 %copy_bitcast_fusion = (bf16[32,16,16,128]{3,2,1,0:T(8,128)(2,1)}, bf16[32,16,16,128]{3,2,1,0:T(8,128)(2,1)}) fusion(bf16[16,32,16,128]{3,2,1,0:T(8,128)(2,1)} %param.5, bf16[16,32,16,128]{3,2,1,0:T(8,128)(2,1)} %param.4), kind=kLoop, calls=%fused_computation | loop fusion | bytes 8388608 | tf_op jit(solution)/shard_map/transpose | solution.py:286
  11.5 43.0 %shard_map.46 = bf16[32,16,16,128]{3,2,1,0:T(8,128)(2,1)S(1)} custom-call(bf16[32,16,16,128]{3,2,1,0:T(8,128)(2,1)} %get-tuple-element.6.g_in, bf16[32,16,16,128]{3,2,1,0:T(8,128)(2,1)} %get-tuple-element.5.p_in, bf16[2304,256]{1,0:T(8,128)(2,1)S(1)} %bitcast.10, bf16[2304,256]{1,0:T(8,128)(2,1)S(1)} %bitcast.11), custom_call_target="tpu_custom_call" | custom-call | flops 9663676416 | bytes 8388608 | tf_op jit(solution)/shard_map/pallas_call | solution.py:289
  54.5 1.9 %copy.9 = bf16[16,32,16,128]{3,2,1,0:T(8,128)(2,1)} copy(bf16[16,32,16,128]{3,0,2,1:T(8,128)(2,1)S(1)} %bitcast.9) | data formatting | bytes 4194304 | tf_op jit(solution)/shard_map/transpose | solution.py:311
Async XLA Ops:
  0.0 1.7 %copy-start = (bf16[3,3,256,256]{3,2,1,0:T(8,128)(2,1)S(1)}, bf16[3,3,256,256]{3,2,1,0:T(8,128)(2,1)}, u32[]{:S(2)}) copy-start(bf16[3,3,256,256]{3,2,1,0:T(8,128)(2,1)} %param.7) | copy-start | bytes 3538948

commit v3 on v2

--- a/solution.py
+++ b/solution.py
@@ -23,7 +23,7 @@
     return jnp.dot(jnp.concatenate(pieces, axis=1), weight[...], preferred_element_type=jnp.float32)
 
 
-def kernel(nrow, ncol, g_in, p_in, w1, w2, out, gbuf, pbuf, hbuf, obuf, gvia, hvia, send, recv, local):
+def kernel(nrow, ncol, g_in, p_in, k1, k2, out, gbuf, pbuf, hbuf, obuf, gvia, hvia, praw, w1, w2, send, recv, local):
     r, c, f = lax.axis_index("row"), lax.axis_index("col"), lax.axis_index("filt")
     o = 1 - f
     rows = g_in.shape[0] // 2
@@ -118,9 +118,15 @@
     mine.start()
     start(has_bot, g_in.at[pl.ds(2 * rows - GS, GS)], gbuf.at[f, pl.ds(0, GS), gcol], T + f, (r + 1, c, 0))
     start(has_top, g_in.at[pl.ds(0, GS)], gbuf.at[f, pl.ds(rows + GS, GS), gcol], B + f, (r - 1, c, 1))
-    start(None, p_in.at[pl.ds(rows * o, rows)], pbuf.at[f], PRE, partner)
-    own_pre = pltpu.make_async_copy(p_in.at[pl.ds(rows * f, rows)], pbuf.at[f], local.at[1])
+    start(None, p_in.at[:, pl.ds(rows * o, rows)], praw.at[f], PRE, partner)
+    own_pre = pltpu.make_async_copy(p_in.at[:, pl.ds(rows * f, rows)], praw.at[f], local.at[1])
     own_pre.start()
+
+    for src, dst in ((k2, w2), (k1, w1)):
+        depth = src.shape[3]
+        for p in range(3):
+            for q in range(3):
+                dst[pl.ds((3 * p + q) * depth, depth)] = src[p, q].T
 
     if folded:
         @pl.when(jnp.logical_or(c == 0, c == 3))
@@ -131,8 +137,13 @@
 
     landed(gbuf.at[o, pl.ds(GS * o, span), gcol], MAIN)
     mine.wait()
-    landed(pbuf.at[o], PRE)
+    landed(praw.at[o], PRE)
     own_pre.wait()
+
+    @pl.loop(0, rows)
+    def _(y):
+        for half in range(2):
+            pbuf[half, y] = jnp.swapaxes(praw[half, :, y], 0, 1)
 
     @pl.when(jnp.logical_and(f == 0, has_top))
     def _():
@@ -282,7 +293,6 @@
 
     def per_device(grad_out, pre_act, weight_one, weight_two):
         batch, rows, cols, chan = grad_out.shape
-        taps = lambda w: jnp.swapaxes(w, 2, 3).reshape(-1, w.shape[2])
         inward = lambda a: jnp.transpose(a, (1, 2, 0, 3))
         strip = rows // 2
         kind = grad_out.dtype
@@ -298,6 +308,9 @@
                 pltpu.VMEM((2, strip, cols, batch, chan), kind),
                 pltpu.VMEM((strip, GS, batch, chan), kind),
                 pltpu.VMEM((2, strip, HS, batch, chan), kind),
+                pltpu.VMEM((2, batch, strip, cols, chan), kind),
+                pltpu.VMEM((9 * 2 * chan, 2 * chan), kind),
+                pltpu.VMEM((9 * 2 * chan, 2 * chan), kind),
                 pltpu.SemaphoreType.DMA((30,)),
                 pltpu.SemaphoreType.DMA((25,)),
                 pltpu.SemaphoreType.DMA((3,)),
@@ -307,7 +320,7 @@
             cost_estimate=pl.CostEstimate(
                 flops=4 * 9 * batch * rows * cols * chan * 2 * chan, bytes_accessed=8 * batch * rows * cols * chan,
                 transcendentals=0),
-        )(inward(grad_out), inward(pre_act), taps(weight_one), taps(weight_two))
+        )(inward(grad_out), pre_act, weight_one, weight_two)
         return jnp.transpose(out, (2, 0, 1, 3))
 
     placed = (P(None, "row", "col", "filt"), P(None, "row", "col", "filt"), P(), P())

time: 56.6 us -> 50.6 us (0.89)
  local copies, waits for them, and re-layouts: 13.4 us -> 7.36 us
    transpose x3 -> x0, local copies, waits for them, and re-layouts: 11.5 us -> none  [the longest x1 9.11 us: per_device(): inward = lambda a: jnp.transpose(a, (1, 2, 0, 3))]
    unnamed x2 -> x5, local copies, waits for them, and re-layouts: 0.01 us -> 5.5 us
where the time goes in v3:
time: 50.6 us; the launch traced here: 50.3 us
  Pallas kernels  43 us (85%)
  local copies, waits for them, and re-layouts  7.36 us (15%)
    pallas_call x1, Pallas kernels, per_device(): pl.pallas_call(functools.partial(kernel, nrow, ncol), out_shape=jax.Shape...  43 us
    unnamed x5, local copies, waits for them, and re-layouts  5.5 us
    transpose x1, local copies, waits for them, and re-layouts, per_device(): return jnp.transpose(out, (2, 0, 1, 3))  1.86 us

profile of v3, /device:TPU:0, one launch (start us, length us, event | category | flops | bytes accessed | tf_op | source)
XLA Modules:
  0.0 50.3 jit_solution(16889395184567721969)
XLA Ops:
  0.0 0.0 copy-start.1
  0.0 0.0 copy-start
  0.0 5.5 %copy.8 = bf16[16,32,16,128]{3,0,2,1:T(8,128)(2,1)} copy(bf16[16,32,16,128]{3,2,1,0:T(8,128)(2,1)} %param.4) | data formatting | bytes 4194304 | tf_op args[0]
  5.5 0.0 copy-done.1
  5.5 0.0 copy-done
  5.5 43.0 %shard_map.46 = bf16[32,16,16,128]{3,2,1,0:T(8,128)(2,1)S(1)} custom-call(bf16[32,16,16,128]{3,2,1,0:T(8,128)(2,1)} %bitcast.5, bf16[16,32,16,128]{3,2,1,0:T(8,128)(2,1)} %p_in.1, bf16[3,3,256,256]{3,2,1,0:T(8,128)(2,1)S(1)} %copy-done, bf16[3,3,256,256]{3,2,1,0:T(8,128)(2,1)S(1)} %copy-done.1), custom_call_target="tpu_custom_call" | custom-call | flops 9663676416 | bytes 8388608 | tf_op jit(solution)/shard_map/pallas_call | solution.py:299
  48.5 1.9 %copy.6 = bf16[16,32,16,128]{3,2,1,0:T(8,128)(2,1)} copy(bf16[16,32,16,128]{3,0,2,1:T(8,128)(2,1)S(1)} %bitcast.4) | data formatting | bytes 4194304 | tf_op jit(solution)/shard_map/transpose | solution.py:324
Async XLA Ops:
  0.0 5.5 %copy-start.1 = (bf16[3,3,256,256]{3,2,1,0:T(8,128)(2,1)S(1)}, bf16[3,3,256,256]{3,2,1,0:T(8,128)(2,1)}, u32[]{:S(2)}) copy-start(bf16[3,3,256,256]{3,2,1,0:T(8,128)(2,1)} %k2.1) | copy-start | bytes 3538948
  0.0 5.5 %copy-start = (bf16[3,3,256,256]{3,2,1,0:T(8,128)(2,1)S(1)}, bf16[3,3,256,256]{3,2,1,0:T(8,128)(2,1)}, u32[]{:S(2)}) copy-start(bf16[3,3,256,256]{3,2,1,0:T(8,128)(2,1)} %k1.1) | copy-start | bytes 3538948

commit v4 on v3

--- a/solution.py
+++ b/solution.py
@@ -23,7 +23,7 @@
     return jnp.dot(jnp.concatenate(pieces, axis=1), weight[...], preferred_element_type=jnp.float32)
 
 
-def kernel(nrow, ncol, g_in, p_in, k1, k2, out, gbuf, pbuf, hbuf, obuf, gvia, hvia, praw, w1, w2, send, recv, local):
+def kernel(nrow, ncol, g_raw, p_in, k1, k2, out, gbuf, pbuf, hbuf, obuf, gvia, hvia, praw, g_in, w1, w2, send, recv, local):
     r, c, f = lax.axis_index("row"), lax.axis_index("col"), lax.axis_index("filt")
     o = 1 - f
     rows = g_in.shape[0] // 2
@@ -71,6 +71,11 @@
     if folded:
         pl.semaphore_signal(barrier, inc=1, device_id=(r, across, f), device_id_type=MESH)
         count = count + 1
+
+    @pl.loop(0, 2 * rows)
+    def _(y):
+        g_in[y] = jnp.swapaxes(g_raw[:, y], 0, 1)
+
     pl.semaphore_wait(barrier, count)
 
     def copy(src, dst, sidx, ridx, device):
@@ -293,13 +298,12 @@
 
     def per_device(grad_out, pre_act, weight_one, weight_two):
         batch, rows, cols, chan = grad_out.shape
-        inward = lambda a: jnp.transpose(a, (1, 2, 0, 3))
         strip = rows // 2
         kind = grad_out.dtype
         out = pl.pallas_call(
             functools.partial(kernel, nrow, ncol),
             out_shape=jax.ShapeDtypeStruct((rows, cols, batch, chan), kind),
-            in_specs=[pl.BlockSpec(memory_space=pl.ANY)] * 2 + [pl.BlockSpec(memory_space=pltpu.VMEM)] * 2,
+            in_specs=[pl.BlockSpec(memory_space=pltpu.VMEM), pl.BlockSpec(memory_space=pl.ANY)] + [pl.BlockSpec(memory_space=pltpu.VMEM)] * 2,
             out_specs=pl.BlockSpec(memory_space=pl.ANY),
             scratch_shapes=[
                 pltpu.VMEM((2, strip + 2 * GS, cols + 2 * GS, batch, chan), kind),
@@ -309,6 +313,7 @@
                 pltpu.VMEM((strip, GS, batch, chan), kind),
                 pltpu.VMEM((2, strip, HS, batch, chan), kind),
                 pltpu.VMEM((2, batch, strip, cols, chan), kind),
+                pltpu.VMEM((rows, cols, batch, chan), kind),
                 pltpu.VMEM((9 * 2 * chan, 2 * chan), kind),
                 pltpu.VMEM((9 * 2 * chan, 2 * chan), kind),
                 pltpu.SemaphoreType.DMA((30,)),
@@ -320,7 +325,7 @@
             cost_estimate=pl.CostEstimate(
                 flops=4 * 9 * batch * rows * cols * chan * 2 * chan, bytes_accessed=8 * batch * rows * cols * chan,
                 transcendentals=0),
-        )(inward(grad_out), pre_act, weight_one, weight_two)
+        )(grad_out, pre_act, weight_one, weight_two)
         return jnp.transpose(out, (2, 0, 1, 3))
 
     placed = (P(None, "row", "col", "filt"), P(None, "row", "col", "filt"), P(), P())

time: 50.6 us -> 49.1 us (0.970)
  local copies, waits for them, and re-layouts: 7.36 us -> 4.4 us
  Pallas kernels: 43 us -> 44.3 us
    unnamed x5 -> x4, local copies, waits for them, and re-layouts: 5.5 us -> 2.54 us
    pallas_call x1, Pallas kernels: 43 us -> 44.3 us  [per_device(): pl.pallas_call(functools.partial(kernel, nrow, ncol), out_shape=jax.Shape...]
where the time goes in v4:
time: 49.1 us; the launch traced here: 48.7 us
  Pallas kernels  44.3 us (90%)
  local copies, waits for them, and re-layouts  4.4 us (9%)
    pallas_call x1, Pallas kernels, per_device(): pl.pallas_call(functools.partial(kernel, nrow, ncol), out_shape=jax.Shape...  44.3 us
    unnamed x4, local copies, waits for them, and re-layouts  2.54 us
    transpose x1, local copies, waits for them, and re-layouts, per_device(): return jnp.transpose(out, (2, 0, 1, 3))  1.86 us

profile of v4, /device:TPU:0, one launch (start us, length us, event | category | flops | bytes accessed | tf_op | source)
XLA Modules:
  0.0 48.7 jit_solution(6478147378755115426)
XLA Ops:
  0.0 0.0 copy-start
  0.0 1.3 %copy-done = bf16[3,3,256,256]{3,2,1,0:T(8,128)(2,1)S(1)} copy-done((bf16[3,3,256,256]{3,2,1,0:T(8,128)(2,1)S(1)}, bf16[3,3,256,256]{3,2,1,0:T(8,128)(2,1)}, u32[]{:S(2)}) %copy-start) | copy-done | bytes 1179672
  1.3 0.0 copy-start.1
  1.3 1.3 %copy-done.1 = bf16[3,3,256,256]{3,2,1,0:T(8,128)(2,1)S(1)} copy-done((bf16[3,3,256,256]{3,2,1,0:T(8,128)(2,1)S(1)}, bf16[3,3,256,256]{3,2,1,0:T(8,128)(2,1)}, u32[]{:S(2)}) %copy-start.1) | copy-done | bytes 1179672
  2.5 44.3 %shard_map.46 = bf16[32,16,16,128]{3,2,1,0:T(8,128)(2,1)S(1)} custom-call(bf16[16,32,16,128]{3,2,1,0:T(8,128)(2,1)} %g_raw.1, bf16[16,32,16,128]{3,2,1,0:T(8,128)(2,1)} %p_in.1, bf16[3,3,256,256]{3,2,1,0:T(8,128)(2,1)S(1)} %copy-done, bf16[3,3,256,256]{3,2,1,0:T(8,128)(2,1)S(1)} %copy-done.1), custom_call_target="tpu_custom_call" | custom-call | flops 9663676416 | bytes 8388608 | tf_op jit(solution)/shard_map/pallas_call | solution.py:303
  46.9 1.9 %copy.5 = bf16[16,32,16,128]{3,2,1,0:T(8,128)(2,1)} copy(bf16[16,32,16,128]{3,0,2,1:T(8,128)(2,1)S(1)} %bitcast.1) | data formatting | bytes 4194304 | tf_op jit(solution)/shard_map/transpose | solution.py:329
Async XLA Ops:
  0.0 1.3 %copy-start = (bf16[3,3,256,256]{3,2,1,0:T(8,128)(2,1)S(1)}, bf16[3,3,256,256]{3,2,1,0:T(8,128)(2,1)}, u32[]{:S(2)}) copy-start(bf16[3,3,256,256]{3,2,1,0:T(8,128)(2,1)} %k1.1) | copy-start | bytes 3538948
  1.3 1.3 %copy-start.1 = (bf16[3,3,256,256]{3,2,1,0:T(8,128)(2,1)S(1)}, bf16[3,3,256,256]{3,2,1,0:T(8,128)(2,1)}, u32[]{:S(2)}) copy-start(bf16[3,3,256,256]{3,2,1,0:T(8,128)(2,1)} %k2.1) | copy-start | bytes 3538948

commit v5 on v4

--- a/solution.py
+++ b/solution.py
@@ -103,6 +103,7 @@
     hrow, hcol = pl.ds(HS, rows), pl.ds(HS, cols)
     L, R, T, B, MAIN, PRE, CORNER, HL, HR, HT, HB, HCORNER, OUT, VIA, HVIA = (
         0, 2, 4, 6, 8, 9, 10, 14, 15, 16, 17, 18, 22, 23, 24)
+    OUTS = (OUT, 25, 26)
 
     if folded:
         start(c == 1, g_in.at[pl.ds(rows, rows), pl.ds(cols - GS, GS)], gvia, VIA, (r, across, f))
@@ -258,6 +259,19 @@
     def _(i):
         result(i * (rows - HS), HS, HS, cols - 2 * HS)
 
+    given = []
+
+    def deliver(part, col, nc):
+        at = pl.ds(col, nc)
+        own = out.at[pl.ds(rows * f, rows), at]
+        ridx = OUTS[part]
+        start(None, obuf.at[o, pl.ds(0, rows), at], own, ridx, partner)
+        keep = pltpu.make_async_copy(obuf.at[f, pl.ds(0, rows), at], own, local.at[2 + part])
+        keep.start()
+        given.append((keep, out.at[pl.ds(rows * o, rows), at], ridx))
+
+    deliver(0, HS, cols - 2 * HS)
+
     @pl.when(has_left)
     def _():
         landed(hbuf.at[both, hrow, pl.ds(0, HS)], HL)
@@ -279,11 +293,11 @@
         result(i * (rows - HS), 0, HS, HS)
         result(i * (rows - HS), cols - HS, HS, HS)
 
-    start(None, obuf.at[o], out.at[pl.ds(rows * f, rows)], OUT, partner)
-    keep = pltpu.make_async_copy(obuf.at[f], out.at[pl.ds(rows * f, rows)], local.at[2])
-    keep.start()
-    landed(out.at[pl.ds(rows * o, rows)], OUT)
-    keep.wait()
+    deliver(1, 0, HS)
+    deliver(2, cols - HS, HS)
+    for keep, theirs, ridx in given:
+        landed(theirs, ridx)
+        keep.wait()
     for there, what in sends:
         if there is None:
             what.wait_send()
@@ -316,9 +330,9 @@
                 pltpu.VMEM((rows, cols, batch, chan), kind),
                 pltpu.VMEM((9 * 2 * chan, 2 * chan), kind),
                 pltpu.VMEM((9 * 2 * chan, 2 * chan), kind),
-                pltpu.SemaphoreType.DMA((30,)),
-                pltpu.SemaphoreType.DMA((25,)),
-                pltpu.SemaphoreType.DMA((3,)),
+                pltpu.SemaphoreType.DMA((32,)),
+                pltpu.SemaphoreType.DMA((27,)),
+                pltpu.SemaphoreType.DMA((5,)),
             ],
             compiler_params=pltpu.CompilerParams(
                 collective_id=0, has_side_effects=True, vmem_limit_bytes=48 * 1024 * 1024),

time: 49.1 us -> 48 us (0.978)
  Pallas kernels: 44.3 us -> 43.3 us
    pallas_call x1, Pallas kernels: 44.3 us -> 43.3 us  [per_device(): pl.pallas_call(functools.partial(kernel, nrow, ncol), out_shape=jax.Shape...]
where the time goes in v5:
time: 48 us; the launch traced here: 47.7 us
  Pallas kernels  43.3 us (90%)
  local copies, waits for them, and re-layouts  4.4 us (9%)
    pallas_call x1, Pallas kernels, per_device(): pl.pallas_call(functools.partial(kernel, nrow, ncol), out_shape=jax.Shape...  43.3 us
    unnamed x4, local copies, waits for them, and re-layouts  2.54 us
    transpose x1, local copies, waits for them, and re-layouts, per_device(): return jnp.transpose(out, (2, 0, 1, 3))  1.86 us

profile of v5, /device:TPU:0, one launch (start us, length us, event | category | flops | bytes accessed | tf_op | source)
XLA Modules:
  0.0 47.7 jit_solution(13599760224918356323)
XLA Ops:
  0.0 0.0 copy-start
  0.0 1.3 %copy-done = bf16[3,3,256,256]{3,2,1,0:T(8,128)(2,1)S(1)} copy-done((bf16[3,3,256,256]{3,2,1,0:T(8,128)(2,1)S(1)}, bf16[3,3,256,256]{3,2,1,0:T(8,128)(2,1)}, u32[]{:S(2)}) %copy-start) | copy-done | bytes 1179672
  1.3 0.0 copy-start.1
  1.3 1.3 %copy-done.1 = bf16[3,3,256,256]{3,2,1,0:T(8,128)(2,1)S(1)} copy-done((bf16[3,3,256,256]{3,2,1,0:T(8,128)(2,1)S(1)}, bf16[3,3,256,256]{3,2,1,0:T(8,128)(2,1)}, u32[]{:S(2)}) %copy-start.1) | copy-done | bytes 1179672
  2.5 43.3 %shard_map.46 = bf16[32,16,16,128]{3,2,1,0:T(8,128)(2,1)S(1)} custom-call(bf16[16,32,16,128]{3,2,1,0:T(8,128)(2,1)} %g_raw.1, bf16[16,32,16,128]{3,2,1,0:T(8,128)(2,1)} %p_in.1, bf16[3,3,256,256]{3,2,1,0:T(8,128)(2,1)S(1)} %copy-done, bf16[3,3,256,256]{3,2,1,0:T(8,128)(2,1)S(1)} %copy-done.1), custom_call_target="tpu_custom_call" | custom-call | flops 9663676416 | bytes 8388608 | tf_op jit(solution)/shard_map/pallas_call | solution.py:317
  45.8 1.9 %copy.5 = bf16[16,32,16,128]{3,2,1,0:T(8,128)(2,1)} copy(bf16[16,32,16,128]{3,0,2,1:T(8,128)(2,1)S(1)} %bitcast.1) | data formatting | bytes 4194304 | tf_op jit(solution)/shard_map/transpose | solution.py:343
Async XLA Ops:
  0.0 1.3 %copy-start = (bf16[3,3,256,256]{3,2,1,0:T(8,128)(2,1)S(1)}, bf16[3,3,256,256]{3,2,1,0:T(8,128)(2,1)}, u32[]{:S(2)}) copy-start(bf16[3,3,256,256]{3,2,1,0:T(8,128)(2,1)} %k1.1) | copy-start | bytes 3538948
  1.3 1.3 %copy-start.1 = (bf16[3,3,256,256]{3,2,1,0:T(8,128)(2,1)S(1)}, bf16[3,3,256,256]{3,2,1,0:T(8,128)(2,1)}, u32[]{:S(2)}) copy-start(bf16[3,3,256,256]{3,2,1,0:T(8,128)(2,1)} %k2.1) | copy-start | bytes 3538948

commit v6 on v5

--- a/solution.py
+++ b/solution.py
@@ -72,7 +72,7 @@
         pl.semaphore_signal(barrier, inc=1, device_id=(r, across, f), device_id_type=MESH)
         count = count + 1
 
-    @pl.loop(0, 2 * rows)
+    @pl.loop(0, 2 * rows, unroll=4)
     def _(y):
         g_in[y] = jnp.swapaxes(g_raw[:, y], 0, 1)
 
@@ -146,7 +146,7 @@
     landed(praw.at[o], PRE)
     own_pre.wait()
 
-    @pl.loop(0, rows)
+    @pl.loop(0, rows, unroll=2)
     def _(y):
         for half in range(2):
             pbuf[half, y] = jnp.swapaxes(praw[half, :, y], 0, 1)

time: 48 us -> 48 us (level)
  no operation moved by 1% of the time
where the time goes in v6:
time: 48 us; the launch traced here: 47.7 us
  Pallas kernels  43.3 us (90%)
  local copies, waits for them, and re-layouts  4.4 us (9%)
    pallas_call x1, Pallas kernels, per_device(): pl.pallas_call(functools.partial(kernel, nrow, ncol), out_shape=jax.Shape...  43.3 us
    unnamed x4, local copies, waits for them, and re-layouts  2.54 us
    transpose x1, local copies, waits for them, and re-layouts, per_device(): return jnp.transpose(out, (2, 0, 1, 3))  1.86 us

profile of v6, /device:TPU:0, one launch (start us, length us, event | category | flops | bytes accessed | tf_op | source)
XLA Modules:
  0.0 47.7 jit_solution(10825637029800029765)
XLA Ops:
  0.0 0.0 copy-start
  0.0 1.3 %copy-done = bf16[3,3,256,256]{3,2,1,0:T(8,128)(2,1)S(1)} copy-done((bf16[3,3,256,256]{3,2,1,0:T(8,128)(2,1)S(1)}, bf16[3,3,256,256]{3,2,1,0:T(8,128)(2,1)}, u32[]{:S(2)}) %copy-start) | copy-done | bytes 1179672
  1.3 0.0 copy-start.1
  1.3 1.3 %copy-done.1 = bf16[3,3,256,256]{3,2,1,0:T(8,128)(2,1)S(1)} copy-done((bf16[3,3,256,256]{3,2,1,0:T(8,128)(2,1)S(1)}, bf16[3,3,256,256]{3,2,1,0:T(8,128)(2,1)}, u32[]{:S(2)}) %copy-start.1) | copy-done | bytes 1179672
  2.5 43.3 %shard_map.46 = bf16[32,16,16,128]{3,2,1,0:T(8,128)(2,1)S(1)} custom-call(bf16[16,32,16,128]{3,2,1,0:T(8,128)(2,1)} %g_raw.1, bf16[16,32,16,128]{3,2,1,0:T(8,128)(2,1)} %p_in.1, bf16[3,3,256,256]{3,2,1,0:T(8,128)(2,1)S(1)} %copy-done, bf16[3,3,256,256]{3,2,1,0:T(8,128)(2,1)S(1)} %copy-done.1), custom_call_target="tpu_custom_call" | custom-call | flops 9663676416 | bytes 8388608 | tf_op jit(solution)/shard_map/pallas_call | solution.py:317
  45.8 1.9 %copy.5 = bf16[16,32,16,128]{3,2,1,0:T(8,128)(2,1)} copy(bf16[16,32,16,128]{3,0,2,1:T(8,128)(2,1)S(1)} %bitcast.1) | data formatting | bytes 4194304 | tf_op jit(solution)/shard_map/transpose | solution.py:343
Async XLA Ops:
  0.0 1.3 %copy-start = (bf16[3,3,256,256]{3,2,1,0:T(8,128)(2,1)S(1)}, bf16[3,3,256,256]{3,2,1,0:T(8,128)(2,1)}, u32[]{:S(2)}) copy-start(bf16[3,3,256,256]{3,2,1,0:T(8,128)(2,1)} %k1.1) | copy-start | bytes 3538948
  1.3 1.3 %copy-start.1 = (bf16[3,3,256,256]{3,2,1,0:T(8,128)(2,1)S(1)}, bf16[3,3,256,256]{3,2,1,0:T(8,128)(2,1)}, u32[]{:S(2)}) copy-start(bf16[3,3,256,256]{3,2,1,0:T(8,128)(2,1)} %k2.1) | copy-start | bytes 3538948
